TPU v7x, 32 devices: a whole 2x2x4 slice. The times are simulated.
32 devices in a mesh: own: 8 (over z, y), red: 4 (over x, core).
Axes of the slice: x: 2, y: 2, z: 4, core: 2. Of those that a mesh axis runs over, the one named last changes fastest.
Arguments:
- amp_tiles: bfloat16 [2048, 128, 128], P(('own', 'red')), may hold values from -6 to 6
- int_tiles: bfloat16 [2048, 128, 128], P(('own', 'red')), may hold values from -0.0625 to 0.0625
- requests: int32 [8, 4, 8, 2, 8], P('own', 'red'), may hold values from -1 to 63, as said below
- tri_amp: int32 [256, 4, 64], P('own', 'red'), may hold values from 0 to 63, as said below
- tri_int: int32 [256, 4, 64], P('own', 'red'), may hold values from 0 to 63, as said below
- tri_count: int32 [256, 4], P('own', 'red'), may hold values from 1 to 64, as said below
Outputs:
- residual: float32 [256, 128, 128], P(('own', 'red'))
Inputs may be any that keep to these rules, and one draw needn't show every extreme that they name: -1 marks an empty slot and live slots come first; the live numbers in one row of 8 slots are distinct; every owner device has 8 live amplitude requests to some holder and 8 live integral requests to some holder. tri_amp[t, r, k] // 8 is a holder h and tri_amp[t, r, k] % 8 is below the number of live amplitude requests of the owner of t, on red index r, to h. `tri_int`: likewise for the integral requests. `tri_count`: on every owner and red index some residual tile has 64 live triples.
All inputs are finite; a program needn't handle non-finite values.
Results may differ from a plain program's by a relative error of at most 0.0003.
Values may be sent and summed in bfloat16 or wider, within the bound.
A program may use at most 128 MiB of HBM per device.

v0:
```python
import functools

import jax
import jax.numpy as jnp
from jax import lax
from jax.experimental import pallas as pl
from jax.experimental.pallas import tpu as pltpu
from jax.sharding import PartitionSpec as P

MESH = pl.DeviceIdType.MESH
CORES = 2
EARLY_PARTS = 2
GROUP = 4
ITEMS = 8


def flip_bits(value, mask):
    bit = 1
    while bit <= mask:
        if mask & bit:
            value = value + (1 - 2 * ((value // bit) % 2)) * bit
        bit *= 2
    return value


def product(amp_list, int_list):
    left = jnp.concatenate(amp_list, axis=1)
    right = jnp.concatenate(int_list, axis=0)
    return jnp.dot(left, right, preferred_element_type=jnp.float32)


def exchange_kernel(
    n_own, n_red, cap, rows, slots,
    req_hbm, amp_hbm, int_hbm, amp_at_hbm, int_at_hbm, count_hbm,
    amp_out, far_int, part, late,
    recv_amp, near_int, req_ref, tri_amp, tri_int, counts, amp_vec, int_vec, asked_vmem, asked_smem, amp_store, int_store, send_amp, send_int,
    req_send, req_recv, local_sem, tile_send, tile_recv,
):
    store = amp_store.shape[0]
    received = n_own * cap
    half_own = n_own // 2
    half_slots = half_own * cap
    me = lax.axis_index("own")
    my_half = me // half_own

    load_amp = pltpu.make_async_copy(amp_hbm, amp_store, local_sem.at[0])
    load_int = pltpu.make_async_copy(int_hbm, int_store, local_sem.at[1])
    load_req = pltpu.make_async_copy(req_hbm, req_ref, local_sem.at[3])
    load_req.start()
    load_amp.start()
    load_int.start()
    loads = []
    for index, (src, dst) in enumerate([
        (amp_at_hbm, tri_amp), (int_at_hbm, tri_int), (count_hbm, counts),
        (amp_at_hbm, amp_vec), (int_at_hbm, int_vec),
    ]):
        load = pltpu.make_async_copy(src, dst, local_sem.at[4 + index])
        load.start()
        loads.append(load)

    barrier = pltpu.get_barrier_semaphore()
    for step in range(1, n_own):
        pl.semaphore_signal(
            barrier, inc=1, device_id={"own": flip_bits(me, step)}, device_id_type=MESH
        )
    pl.semaphore_wait(barrier, n_own - 1)

    load_req.wait()
    asks = []
    for step in range(n_own - 1, 0, -1):
        peer = flip_bits(me, step)
        copy = pltpu.make_async_remote_copy(
            src_ref=req_ref.at[peer],
            dst_ref=asked_vmem.at[me],
            send_sem=req_send.at[step],
            recv_sem=req_recv.at[step],
            device_id={"own": peer},
            device_id_type=MESH,
        )
        copy.start()
        asks.append(copy)
    asked_vmem[me] = req_ref[me]
    for copy in asks:
        copy.wait()
    to_smem = pltpu.make_async_copy(asked_vmem, asked_smem, local_sem.at[2])
    to_smem.start()
    to_smem.wait()

    far = list(range(n_own - 1, half_own - 1, -1))
    near = list(range(half_own - 1, 0, -1))
    order = []
    for index, step in enumerate(far):
        order.append((0, step))
        if index < len(near):
            order.append((0, near[index]))
    for index, step in enumerate(far):
        if index < len(near):
            order.append((1, near[index]))
        order.append((1, step))

    def pack(kind, step, slot):
        peer = flip_bits(me, step)
        number = asked_smem[peer, kind, slot]
        source = (amp_store, int_store)[kind]
        tile = source[jnp.clip(number, 0, store - 1)]
        return tile.T if kind == 1 else tile

    my_place = (me % half_own) * cap
    recv_amp[received] = jnp.zeros_like(recv_amp[received])
    loaded = [False, False]
    copies = {}
    for kind, step in order:
        if not loaded[kind]:
            (load_amp, load_int)[kind].wait()
            loaded[kind] = True
        outbox = (send_amp, send_int)[kind]
        for slot in range(cap):
            outbox[step, slot] = pack(kind, step, slot)
        if kind == 0:
            inbox = recv_amp.at[pl.ds(me * cap, cap)]
        elif step >= half_own:
            inbox = far_int.at[pl.ds(my_place, cap)]
        else:
            inbox = near_int.at[pl.ds(my_place, cap)]
        copy = pltpu.make_async_remote_copy(
            src_ref=outbox.at[step],
            dst_ref=inbox,
            send_sem=tile_send.at[kind, step],
            recv_sem=tile_recv.at[kind, step],
            device_id={"own": flip_bits(me, step)},
            device_id_type=MESH,
        )
        copy.start()
        copies[kind, step] = copy
    for slot in range(cap):
        recv_amp[me * cap + slot] = pack(0, 0, slot)
        near_int[my_place + slot] = pack(1, 0, slot)

    for load in loads:
        load.wait()

    wide = late.shape[-1]
    row_at = lax.broadcasted_iota(jnp.int32, (rows, slots), 0)
    slot_at = lax.broadcasted_iota(jnp.int32, (rows, slots), 1)
    live = jnp.zeros((rows, slots), jnp.int32)
    for row in range(rows):
        live = jnp.where(row_at == row, counts[row], live)
    amp_at = amp_vec[:, 0, :]
    int_at = int_vec[:, 0, :]
    is_late = (slot_at < live) & ((int_at // half_slots) != my_half)
    late_one = jnp.where(is_late, 1.0, 0.0).astype(jnp.float32)
    before = jnp.where(
        lax.broadcasted_iota(jnp.int32, (slots, slots), 0)
        < lax.broadcasted_iota(jnp.int32, (slots, slots), 1),
        1.0, 0.0,
    ).astype(jnp.float32)
    rank = jnp.dot(late_one, before, preferred_element_type=jnp.float32).astype(jnp.int32)
    rank = jnp.where(is_late, rank, wide)
    place = lax.broadcasted_iota(jnp.int32, (rows, wide), 1)
    total = jnp.sum(late_one, axis=1, keepdims=True).astype(jnp.int32)
    amp_list = jnp.where(place == slots, total, received)
    int_list = jnp.zeros((rows, wide), jnp.int32)
    int_far = int_at % half_slots
    for k in range(slots):
        here = place == rank[:, k : k + 1]
        amp_list = jnp.where(here, amp_at[:, k : k + 1], amp_list)
        int_list = jnp.where(here, int_far[:, k : k + 1], int_list)
    late[0] = amp_list
    late[1] = int_list

    blocks = (total + (GROUP - 1)) // GROUP
    group_at = lax.broadcasted_iota(jnp.int32, (rows, 1), 0) // (rows // n_red)
    blocks = jnp.where(group_at == lax.axis_index("red"), 0, blocks).astype(jnp.float32)
    lower = jnp.where(
        lax.broadcasted_iota(jnp.int32, (rows, rows), 1)
        < lax.broadcasted_iota(jnp.int32, (rows, rows), 0),
        1.0, 0.0,
    ).astype(jnp.float32)
    ahead = jnp.dot(
        lower, jnp.broadcast_to(blocks, (rows, wide)), preferred_element_type=jnp.float32
    ).astype(jnp.int32)
    item_count = jnp.sum(blocks).astype(jnp.int32)
    item_rows = rows * slots // GROUP // wide
    for line in range(item_rows):
        item = lax.broadcasted_iota(jnp.int32, (rows, wide), 1) + line * wide
        begun = ahead <= item
        row_of = jnp.sum(begun.astype(jnp.int32), axis=0, keepdims=True) - 1
        start = jnp.max(jnp.where(begun, ahead, 0), axis=0, keepdims=True)
        first_of = (item[:1] - start) * GROUP
        listed = item[:1] < item_count
        late[2, line : line + 1] = jnp.where(listed, row_of, 0)
        late[2, item_rows + line : item_rows + line + 1] = jnp.where(
            listed, first_of, slots + GROUP
        )
    late[2, 2 * item_rows : 2 * item_rows + 1] = jnp.broadcast_to(item_count, (1, wide))

    for kind, step in order:
        if kind == 0 or step < half_own:
            copies[kind, step].wait_recv()
    keep_amp = pltpu.make_async_copy(recv_amp, amp_out, local_sem.at[9])
    keep_amp.start()

    def one_row(row, carry):
        count = counts[row]
        total = None
        for piece in range(EARLY_PARTS):
            amps, ints = [], []
            for k in range(slots // EARLY_PARTS):
                slot = piece * (slots // EARLY_PARTS) + k
                at = tri_int[row, 0, slot]
                early = ((at // half_slots) == my_half) & (slot < count)
                amps.append(recv_amp[jnp.where(early, tri_amp[row, 0, slot], received)])
                ints.append(near_int[at % half_slots])
            value = product(amps, ints)
            total = value if total is None else total + value
        part[row] = total
        return carry

    lax.fori_loop(0, rows, one_row, 0)

    for kind, step in order:
        if kind == 1 and step >= half_own:
            copies[kind, step].wait_recv()
    for kind, step in order:
        copies[kind, step].wait_send()
    keep_amp.wait()


def late_kernel(rows, slots, late, recv_amp, far_int, part, out):
    wide = late.shape[-1]
    item_rows = rows * slots // GROUP // wide

    def some(block, carry):
        found = []
        for index in range(ITEMS):
            item = block * ITEMS + index
            line, column = item // wide, item % wide
            row = late[2, line, column]
            first = late[2, item_rows + line, column]
            amps = [recv_amp[late[0, row, first + k]] for k in range(GROUP)]
            ints = [far_int[late[1, row, first + k]] for k in range(GROUP)]
            found.append((row, product(amps, ints)))
        for row, value in found:
            out[row] += value
        return carry

    items = late[2, 2 * item_rows, 0]
    lax.fori_loop(0, (items + ITEMS - 1) // ITEMS, some, 0)


def scatter_kernel(
    n_red, slots, late, recv_amp, far_int, part,
    out_ref, listed, mid, sib, across, list_sem, sib_send, sib_recv, across_send, across_recv
):
    n_x = n_red // CORES
    per_dev = part.shape[0] // n_red
    red = lax.axis_index("red")
    my_x, my_core = red // CORES, red % CORES
    sibling = my_x * CORES + (1 - my_core)
    load_list = pltpu.make_async_copy(late.at[pl.ds(0, 2)], listed, list_sem)
    load_list.start()

    barrier = pltpu.get_barrier_semaphore()
    pl.semaphore_signal(barrier, inc=1, device_id={"red": sibling}, device_id_type=MESH)
    for step in range(1, n_x):
        peer = ((my_x + step) % n_x) * CORES + my_core
        pl.semaphore_signal(barrier, inc=1, device_id={"red": peer}, device_id_type=MESH)
    pl.semaphore_wait(barrier, n_x)

    def to_sibling(step, j):
        x = (my_x + step) % n_x
        return pltpu.make_async_remote_copy(
            src_ref=part.at[(x * CORES + (1 - my_core)) * per_dev + j],
            dst_ref=sib.at[step, j],
            send_sem=sib_send.at[step, j],
            recv_sem=sib_recv.at[step, j],
            device_id={"red": sibling},
            device_id_type=MESH,
        )

    def to_across(step, j):
        x = (my_x + step) % n_x
        return pltpu.make_async_remote_copy(
            src_ref=mid.at[step - 1, j],
            dst_ref=across.at[step - 1, j],
            send_sem=across_send.at[step - 1, j],
            recv_sem=across_recv.at[step - 1, j],
            device_id={"red": x * CORES + my_core},
            device_id_type=MESH,
        )

    order = list(range(1, n_x)) + [0]
    for step in order:
        for j in range(per_dev):
            to_sibling(step, j).start()
    for step in range(1, n_x):
        x = (my_x + step) % n_x
        for j in range(per_dev):
            to_sibling(step, j).wait_recv()
            row = (x * CORES + my_core) * per_dev + j
            mid[step - 1, j] = part[row] + sib[step, j]
            to_across(step, j).start()

    load_list.wait()

    def own_row(j, carry):
        row = red * per_dev + j
        total = part[row]
        for piece in range(EARLY_PARTS):
            share = slots // EARLY_PARTS
            places = range(piece * share, (piece + 1) * share)
            amps = [recv_amp[listed[0, row, k]] for k in places]
            ints = [far_int[listed[1, row, k]] for k in places]
            total = total + product(amps, ints)
        out_ref[j] = total
        return carry

    lax.fori_loop(0, per_dev, own_row, 0)
    for j in range(per_dev):
        to_sibling(0, j).wait_recv()
        out_ref[j] += sib[0, j]
    for step in range(1, n_x):
        for j in range(per_dev):
            to_across(step, j).wait_recv()
            out_ref[j] += across[step - 1, j]
    for step in order:
        for j in range(per_dev):
            to_sibling(step, j).wait_send()
            if step:
                to_across(step, j).wait_send()


def body(n_own, n_red, amp_tiles, int_tiles, requests, tri_amp, tri_int, tri_count):
    rows, _, slots = tri_amp.shape
    cap = requests.shape[-1]
    tile = amp_tiles.shape[1:]
    store = amp_tiles.shape[0]
    received = n_own * cap
    n_x = n_red // CORES
    per_dev = rows // n_red
    kind = amp_tiles.dtype
    vmem = pl.BlockSpec(memory_space=pltpu.VMEM)
    smem = pl.BlockSpec(memory_space=pltpu.SMEM)
    hbm = pl.BlockSpec(memory_space=pltpu.HBM)
    dma = pltpu.SemaphoreType.DMA
    shape = jax.ShapeDtypeStruct
    partial = shape((rows,) + tile, jnp.float32)
    counts = tri_count.reshape(rows)
    recv_amp, far_int, early, late = pl.pallas_call(
        functools.partial(exchange_kernel, n_own, n_red, cap, rows, slots),
        out_shape=[
            shape((received + 1,) + tile, kind),
            shape((received // 2,) + tile, kind),
            partial,
            shape((3, rows, 2 * slots), jnp.int32),
        ],
        in_specs=[hbm] * 6,
        out_specs=[hbm, vmem, vmem, vmem],
        scratch_shapes=[
            pltpu.VMEM((received + 1,) + tile, kind),
            pltpu.VMEM((received // 2,) + tile, kind),
            pltpu.VMEM((n_own, 2, cap), jnp.int32),
            pltpu.SMEM((rows, 1, slots), jnp.int32),
            pltpu.SMEM((rows, 1, slots), jnp.int32),
            pltpu.SMEM((rows,), jnp.int32),
            pltpu.VMEM((rows, 1, slots), jnp.int32),
            pltpu.VMEM((rows, 1, slots), jnp.int32),
            pltpu.VMEM((n_own, 2, cap), jnp.int32),
            pltpu.SMEM((n_own, 2, cap), jnp.int32),
            pltpu.VMEM((store,) + tile, kind),
            pltpu.VMEM((store,) + tile, kind),
            pltpu.VMEM((n_own, cap) + tile, kind),
            pltpu.VMEM((n_own, cap) + tile, kind),
            dma((n_own,)),
            dma((n_own,)),
            dma((10,)),
            dma((2, n_own)),
            dma((2, n_own)),
        ],
        compiler_params=pltpu.CompilerParams(
            collective_id=0, has_side_effects=True, vmem_limit_bytes=50 * 2**20
        ),
    )(requests[0, 0], amp_tiles, int_tiles, tri_amp, tri_int, counts)
    summed = pl.pallas_call(
        functools.partial(late_kernel, rows, slots),
        out_shape=partial,
        in_specs=[smem, vmem, vmem, vmem],
        out_specs=vmem,
        input_output_aliases={3: 0},
        compiler_params=pltpu.CompilerParams(vmem_limit_bytes=32 * 2**20),
    )(late, recv_amp, far_int, early)
    return pl.pallas_call(
        functools.partial(scatter_kernel, n_red, slots),
        out_shape=shape((per_dev,) + tile, jnp.float32),
        in_specs=[vmem] * 4,
        out_specs=vmem,
        scratch_shapes=[
            pltpu.SMEM((2, rows, 2 * slots), jnp.int32),
            pltpu.VMEM((n_x - 1, per_dev) + tile, jnp.float32),
            pltpu.VMEM((n_x, per_dev) + tile, jnp.float32),
            pltpu.VMEM((n_x - 1, per_dev) + tile, jnp.float32),
            dma,
            dma((n_x, per_dev)),
            dma((n_x, per_dev)),
            dma((n_x - 1, per_dev)),
            dma((n_x - 1, per_dev)),
        ],
        compiler_params=pltpu.CompilerParams(
            collective_id=1, has_side_effects=True, vmem_limit_bytes=32 * 2**20
        ),
    )(late, recv_amp, far_int, summed)


def solution(mesh):
    placed = (
        P(("own", "red"), None, None),
        P(("own", "red"), None, None),
        P("own", "red", None, None, None),
        P("own", "red", None),
        P("own", "red", None),
        P("own", "red"),
    )
    return jax.shard_map(
        functools.partial(body, mesh.shape["own"], mesh.shape["red"]),
        mesh=mesh,
        in_specs=placed,
        out_specs=P(("own", "red"), None, None),
        check_vma=False,
    )
```

profile of v0, /device:TPU:0, one launch (start us, length us, event | category | flops | bytes accessed | tf_op | source)
XLA Modules:
  0.0 128.4 jit_solution(11558612292374047581)
XLA Ops:
  0.0 0.0 copy-start.1
  0.0 0.7 copy-done.1
  0.7 0.0 copy-start.2
  0.7 0.7 copy-done.2
  1.4 0.0 copy-start.3
  1.4 0.7 copy-done.3
  2.1 0.0 copy-start.4
  2.1 0.7 copy-done.4
  2.8 102.4 %shard_map.64 = (bf16[65,128,128]{2,1,0:T(8,128)(2,1)}, bf16[32,128,128]{2,1,0:T(8,128)(2,1)S(1)}, f32[32,128,128]{2,1,0:T(8,128)S(1)}, s32[3,32,128]{2,1,0:T(8,128)S(1)}) custom-call(s32[8,2,8]{2,1,0:T(2,128)S(1)} %bitcast.2, bf16[64,128,128]{2,1,0:T(8,128)(2,1)} %amp_hbm.1, bf16[64,128,128]{2,1,0:T(8,128)(2,1)} %int_hbm.1, s32[32,1,64]{2,1,0:T(1,128)S(1)} %copy-done.1, ...), custom_call_target="tpu_custom_call" | custom-call | tf_op jit(solution)/shard_map/pallas_call | solution.py:349
  105.2 0.0 copy-start
  105.2 1.6 %copy-done = bf16[65,128,128]{2,1,0:T(8,128)(2,1)S(1)} copy-done((bf16[65,128,128]{2,1,0:T(8,128)(2,1)S(1)}, bf16[65,128,128]{2,1,0:T(8,128)(2,1)}, u32[]{:S(2)}) %copy-start) | copy-done | bytes 2129944
  106.8 3.6 %shard_map.65.part = f32[32,128,128]{2,1,0:T(8,128)S(1)} custom-call(s32[3,32,128]{2,1,0:T(8,128)S(1)} %get-tuple-element.9.late, bf16[65,128,128]{2,1,0:T(8,128)(2,1)S(1)} %copy-done, bf16[32,128,128]{2,1,0:T(8,128)(2,1)S(1)} %get-tuple-element.11.far_int, f32[32,128,128]{2,1,0:T(8,128)S(1)} %get-tuple-element.12.part), custom_call_target="tpu_custom_call", output_to_operand_aliasing={{}: (3, {})} | custom-call | tf_op jit(solution)/shard_map/pallas_call | solution.py:384
  110.4 17.2 %shard_map.66 = f32[8,128,128]{2,1,0:T(8,128)S(1)} custom-call(s32[3,32,128]{2,1,0:T(8,128)S(1)} %get-tuple-element.9.late, bf16[65,128,128]{2,1,0:T(8,128)(2,1)S(1)} %copy-done, bf16[32,128,128]{2,1,0:T(8,128)(2,1)S(1)} %get-tuple-element.11.far_int, f32[32,128,128]{2,1,0:T(8,128)S(1)} %shard_map.65.part), custom_call_target="tpu_custom_call" | custom-call | tf_op jit(solution)/shard_map/pallas_call | solution.py:392
  127.6 0.8 copy.13
Async XLA Ops:
  0.0 0.7 copy-start.1
  0.7 0.7 copy-start.2
  1.4 0.7 copy-start.3
  2.1 0.7 copy-start.4
  105.2 1.6 %copy-start = (bf16[65,128,128]{2,1,0:T(8,128)(2,1)S(1)}, bf16[65,128,128]{2,1,0:T(8,128)(2,1)}, u32[]{:S(2)}) copy-start(bf16[65,128,128]{2,1,0:T(8,128)(2,1)} %get-tuple-element.10.recv_amp) | copy-start | bytes 6389764
where the time goes:
time: 129 us; the launch traced here: 128 us
  Pallas kernels  123 us (95%)
  local copies, waits for them, and re-layouts  5.17 us (4%)
    pallas_call x1, Pallas kernels, body(): pl.pallas_call(functools.partial(exchange_kernel, n_own, n_red, cap, rows...  102 us
    pallas_call x1, Pallas kernels, body(): pl.pallas_call(functools.partial(scatter_kernel, n_red, slots), out_shape...  17.2 us
    unnamed x11, local copies, waits for them, and re-layouts  5.17 us
    pallas_call x1, Pallas kernels, body(): pl.pallas_call(functools.partial(late_kernel, rows, slots), out_shape=par...  3.65 us

commit v1 on v0

--- a/solution.py
+++ b/solution.py
@@ -34,7 +34,7 @@
     req_hbm, amp_hbm, int_hbm, amp_at_hbm, int_at_hbm, count_hbm,
     amp_out, far_int, part, late,
     recv_amp, near_int, req_ref, tri_amp, tri_int, counts, amp_vec, int_vec, asked_vmem, asked_smem, amp_store, int_store, send_amp, send_int,
-    req_send, req_recv, local_sem, tile_send, tile_recv,
+    req_send, req_recv, local_sem, list_sem, tile_send, tile_recv,
 ):
     store = amp_store.shape[0]
     received = n_own * cap
@@ -80,11 +80,17 @@
         copy.start()
         asks.append(copy)
     asked_vmem[me] = req_ref[me]
-    for copy in asks:
-        copy.wait()
-    to_smem = pltpu.make_async_copy(asked_vmem, asked_smem, local_sem.at[2])
-    to_smem.start()
-    to_smem.wait()
+    asks = dict(zip(range(n_own - 1, 0, -1), asks))
+
+    def read_ask(step):
+        if step:
+            asks[step].wait_recv()
+        row = pl.ds(flip_bits(me, step), 1)
+        to_smem = pltpu.make_async_copy(
+            asked_vmem.at[row], asked_smem.at[row], list_sem.at[step]
+        )
+        to_smem.start()
+        to_smem.wait()
 
     far = list(range(n_own - 1, half_own - 1, -1))
     near = list(range(half_own - 1, 0, -1))
@@ -114,6 +120,8 @@
             (load_amp, load_int)[kind].wait()
             loaded[kind] = True
         outbox = (send_amp, send_int)[kind]
+        if kind == 0:
+            read_ask(step)
         for slot in range(cap):
             outbox[step, slot] = pack(kind, step, slot)
         if kind == 0:
@@ -132,6 +140,7 @@
         )
         copy.start()
         copies[kind, step] = copy
+    read_ask(0)
     for slot in range(cap):
         recv_amp[me * cap + slot] = pack(0, 0, slot)
         near_int[my_place + slot] = pack(1, 0, slot)
@@ -223,10 +232,14 @@
             copies[kind, step].wait_recv()
     for kind, step in order:
         copies[kind, step].wait_send()
+        if kind == 0:
+            asks[step].wait_send()
     keep_amp.wait()
 
 
-def late_kernel(rows, slots, late, recv_amp, far_int, part, out):
+def late_kernel(rows, slots, late, amp_hbm, far_int, part, out, recv_amp, amp_sem):
+    load_amp = pltpu.make_async_copy(amp_hbm, recv_amp, amp_sem)
+    load_amp.start()
     wide = late.shape[-1]
     item_rows = rows * slots // GROUP // wide
 
@@ -245,12 +258,13 @@
         return carry
 
     items = late[2, 2 * item_rows, 0]
+    load_amp.wait()
     lax.fori_loop(0, (items + ITEMS - 1) // ITEMS, some, 0)
 
 
 def scatter_kernel(
-    n_red, slots, late, recv_amp, far_int, part,
-    out_ref, listed, mid, sib, across, list_sem, sib_send, sib_recv, across_send, across_recv
+    n_red, slots, late, amp_hbm, far_int, part,
+    out_ref, recv_amp, listed, mid, sib, across, list_sem, amp_sem, sib_send, sib_recv, across_send, across_recv
 ):
     n_x = n_red // CORES
     per_dev = part.shape[0] // n_red
@@ -259,6 +273,8 @@
     sibling = my_x * CORES + (1 - my_core)
     load_list = pltpu.make_async_copy(late.at[pl.ds(0, 2)], listed, list_sem)
     load_list.start()
+    load_amp = pltpu.make_async_copy(amp_hbm, recv_amp, amp_sem)
+    load_amp.start()
 
     barrier = pltpu.get_barrier_semaphore()
     pl.semaphore_signal(barrier, inc=1, device_id={"red": sibling}, device_id_type=MESH)
@@ -302,6 +318,7 @@
             to_across(step, j).start()
 
     load_list.wait()
+    load_amp.wait()
 
     def own_row(j, carry):
         row = red * per_dev + j
@@ -374,6 +391,7 @@
             dma((n_own,)),
             dma((n_own,)),
             dma((10,)),
+            dma((n_own,)),
             dma((2, n_own)),
             dma((2, n_own)),
         ],
@@ -384,21 +402,24 @@
     summed = pl.pallas_call(
         functools.partial(late_kernel, rows, slots),
         out_shape=partial,
-        in_specs=[smem, vmem, vmem, vmem],
+        in_specs=[smem, hbm, vmem, vmem],
         out_specs=vmem,
+        scratch_shapes=[pltpu.VMEM((received + 1,) + tile, kind), dma],
         input_output_aliases={3: 0},
-        compiler_params=pltpu.CompilerParams(vmem_limit_bytes=32 * 2**20),
+        compiler_params=pltpu.CompilerParams(vmem_limit_bytes=50 * 2**20),
     )(late, recv_amp, far_int, early)
     return pl.pallas_call(
         functools.partial(scatter_kernel, n_red, slots),
         out_shape=shape((per_dev,) + tile, jnp.float32),
-        in_specs=[vmem] * 4,
+        in_specs=[vmem, hbm, vmem, vmem],
         out_specs=vmem,
         scratch_shapes=[
+            pltpu.VMEM((received + 1,) + tile, kind),
             pltpu.SMEM((2, rows, 2 * slots), jnp.int32),
             pltpu.VMEM((n_x - 1, per_dev) + tile, jnp.float32),
             pltpu.VMEM((n_x, per_dev) + tile, jnp.float32),
             pltpu.VMEM((n_x - 1, per_dev) + tile, jnp.float32),
+            dma,
             dma,
             dma((n_x, per_dev)),
             dma((n_x, per_dev)),
@@ -406,7 +427,7 @@
             dma((n_x - 1, per_dev)),
         ],
         compiler_params=pltpu.CompilerParams(
-            collective_id=1, has_side_effects=True, vmem_limit_bytes=32 * 2**20
+            collective_id=1, has_side_effects=True, vmem_limit_bytes=50 * 2**20
         ),
     )(late, recv_amp, far_int, summed)
 

time: 129 us -> 128 us (level)
  Pallas kernels: 123 us -> 125 us
  local copies, waits for them, and re-layouts: 5.17 us -> 3.58 us
    pallas_call x1, Pallas kernels: 102 us -> 100 us  [body(): pl.pallas_call(functools.partial(exchange_kernel, n_own, n_red, cap, rows...]
    pallas_call x1, Pallas kernels: 3.65 us -> 5.65 us  [body(): pl.pallas_call(functools.partial(late_kernel, rows, slots), out_shape=par...]
    pallas_call x1, Pallas kernels: 17.2 us -> 19 us  [body(): pl.pallas_call(functools.partial(scatter_kernel, n_red, slots), out_shape...]
    unnamed x11 -> x9, local copies, waits for them, and re-layouts: 5.17 us -> 3.58 us
where the time goes in v1:
time: 128 us; the launch traced here: 129 us
  Pallas kernels  125 us (98%)
  local copies, waits for them, and re-layouts  3.58 us (3%)
    pallas_call x1, Pallas kernels, body(): pl.pallas_call(functools.partial(exchange_kernel, n_own, n_red, cap, rows...  100 us
    pallas_call x1, Pallas kernels, body(): pl.pallas_call(functools.partial(scatter_kernel, n_red, slots), out_shape...  19 us
    pallas_call x1, Pallas kernels, body(): pl.pallas_call(functools.partial(late_kernel, rows, slots), out_shape=par...  5.65 us
    unnamed x9, local copies, waits for them, and re-layouts  3.58 us

profile of v1, /device:TPU:0, one launch (start us, length us, event | category | flops | bytes accessed | tf_op | source)
XLA Modules:
  0.0 128.6 jit_solution(6459352770480849830)
XLA Ops:
  0.0 0.0 copy-start
  0.0 0.7 copy-done
  0.7 0.0 copy-start.1
  0.7 0.7 copy-done.1
  1.4 0.0 copy-start.2
  1.4 0.7 copy-done.2
  2.1 0.0 copy-start.3
  2.1 0.7 copy-done.3
  2.8 100.3 %shard_map.64 = (bf16[65,128,128]{2,1,0:T(8,128)(2,1)}, bf16[32,128,128]{2,1,0:T(8,128)(2,1)S(1)}, f32[32,128,128]{2,1,0:T(8,128)S(1)}, s32[3,32,128]{2,1,0:T(8,128)S(1)}) custom-call(s32[8,2,8]{2,1,0:T(2,128)S(1)} %bitcast.2, bf16[64,128,128]{2,1,0:T(8,128)(2,1)} %amp_hbm.1, bf16[64,128,128]{2,1,0:T(8,128)(2,1)} %int_hbm.1, s32[32,1,64]{2,1,0:T(1,128)S(1)} %copy-done, ...), custom_call_target="tpu_custom_call" | custom-call | tf_op jit(solution)/shard_map/pallas_call | solution.py:366
  103.1 5.6 %shard_map.65.part = f32[32,128,128]{2,1,0:T(8,128)S(1)} custom-call(s32[3,32,128]{2,1,0:T(8,128)S(1)} %get-tuple-element.9.late, bf16[65,128,128]{2,1,0:T(8,128)(2,1)} %get-tuple-element.10.amp_hbm, bf16[32,128,128]{2,1,0:T(8,128)(2,1)S(1)} %get-tuple-element.11.far_int, f32[32,128,128]{2,1,0:T(8,128)S(1)} %get-tuple-element.12.part), custom_call_target="tpu_custom_call", output_to_operand_aliasing={{}: (3, {})} | custom-call | tf_op jit(solution)/shard_map/pallas_call | solution.py:402
  108.8 19.0 %shard_map.66 = f32[8,128,128]{2,1,0:T(8,128)S(1)} custom-call(s32[3,32,128]{2,1,0:T(8,128)S(1)} %get-tuple-element.9.late, bf16[65,128,128]{2,1,0:T(8,128)(2,1)} %get-tuple-element.10.amp_hbm, bf16[32,128,128]{2,1,0:T(8,128)(2,1)S(1)} %get-tuple-element.11.far_int, f32[32,128,128]{2,1,0:T(8,128)S(1)} %shard_map.65.part), custom_call_target="tpu_custom_call" | custom-call | tf_op jit(solution)/shard_map/pallas_call | solution.py:411
  127.8 0.8 copy.13
Async XLA Ops:
  0.0 0.7 copy-start
  0.7 0.7 copy-start.1
  1.4 0.7 copy-start.2
  2.1 0.7 copy-start.3
